TPU v7x, 32 devices: a whole 2x2x4 slice. The times are simulated.
32 devices in a mesh: seq: 8 (over z, y), head: 4 (over x, core).
Axes of the slice: x: 2, y: 2, z: 4, core: 2. Of those that a mesh axis runs over, the one named last changes fastest.
Arguments:
- mamba_inner: bfloat16 [1024, 3072], P('seq', 'head'), may hold values from -6 to 6
- mamba_groups: bfloat16 [1024, 512], P('seq'), may hold values from -6 to 6
- selective_gate: bfloat16 [1024, 3072], P('seq', 'head'), may hold values from -6 to 6
- step_raw: float32 [48, 1024], P('head', 'seq'), may hold values from -3 to 3
- step_bias: float32 [48], P('head'), may hold values from -0.5 to 0.5
- decay_log: float32 [48], P('head'), may hold values from -12 to -2
- conv_inner: float32 [4, 3072], P(None, 'head'), may hold values from -3 to 3
- conv_groups: float32 [4, 512], replicated, may hold values from -3 to 3
- gated_norm_gain: float32 [3072], P('head'), may hold values from 0.1 to 1.9
- query_rows: bfloat16 [1024, 1024], P('seq', 'head'), may hold values from -8 to 8
- key_rows: bfloat16 [1024, 256], P('seq'), may hold values from -8 to 8
- value_rows: bfloat16 [1024, 256], P('seq'), may hold values from -6 to 6
- segment_ids: int32 [1024], P('seq'), may hold values from 0 to 15, never falling along the last dimension, each value on 1 to 682 neighbouring positions
- mamba_proj: bfloat16 [3072, 2048], P('head'), may hold values from -0.109375 to 0.109375
- attn_proj: bfloat16 [1024, 2048], P('head'), may hold values from -0.1875 to 0.1875
Outputs:
- mixed: bfloat16 [1024, 2048], P('seq', 'head')
Inputs may be any that keep to these rules, and one draw needn't show every extreme that they name: `segment_ids`: prompt numbers never fall along the tokens; each prompt holds 1 to 682 tokens and one holds exactly 682.
All inputs are finite; a program needn't handle non-finite values.
Results may differ from a plain program's by a relative error of at most 0.015.
Values may be sent and summed in bfloat16 or wider, within the bound.
A program may use at most 128 MiB of HBM per device.

v0:
```python
import math
import jax
import jax.numpy as jnp
from jax import lax
from jax.sharding import PartitionSpec as P

HEAD_CHANNELS = 64
STATE_SIZE = 256
QH = 8
KVH = 2
HD = 128


def shifted(value, axis, steps):
    count = lax.axis_size(axis)
    first, last = (max(0, -steps), min(count, count - steps))
    return lax.ppermute(value, axis, [(source, source + steps) for source in range(first, last)])


def entering(array, axis, combine, identity):
    length, position = (lax.axis_size(axis), lax.axis_index(axis))
    everything = jax.tree.map(
        lambda part, kind: lax.all_gather(part.astype(kind), axis),
        array,
        (jnp.bfloat16, jnp.bfloat16),
    )
    start = jax.tree.map(
        lambda part, zero: jnp.broadcast_to(jnp.asarray(zero, part.dtype), part.shape),
        array,
        identity,
    )

    def turn(k, before):
        reached = k < position
        new = combine(
            before, jax.tree.map(lambda part, own: part[k].astype(own.dtype), everything, array)
        )
        return jax.tree.map(lambda a, b: jnp.where(reached, a, b), new, before)

    return lax.fori_loop(0, length, turn, start)


def conv_silu(rows, weight, segs, rim_rows, rim_segs):
    item_count = rows.shape[0]
    padded = jnp.concatenate([rim_rows.astype(jnp.float32), rows.astype(jnp.float32)], 0)
    seg_pad = jnp.concatenate([rim_segs, segs], 0)
    total = jnp.zeros(rows.shape, jnp.float32)
    for offset in range(weight.shape[0]):
        window = padded[offset : offset + item_count]
        keep = (seg_pad[offset : offset + item_count] == segs).astype(jnp.float32)
        total = total + weight[offset][None, :] * window * keep[:, None]
    return jax.nn.silu(total).astype(jnp.bfloat16)


def mamba_local(inner, groups, segs, steps, rates, prev_last):
    highest = lax.Precision.HIGHEST
    cumul = jnp.cumsum(-steps * rates[:, None], axis=1)
    read_b = groups[:, :STATE_SIZE]
    read_c = groups[:, STATE_SIZE:]
    intersection = jnp.dot(read_c, read_b.T, preferred_element_type=jnp.float32)
    order = jnp.arange(segs.shape[0], dtype=jnp.int32)
    live = (segs[:, None] == segs[None, :]) & (order[:, None] >= order[None, :])
    decays = jnp.exp(jnp.where(live[None], cumul[:, :, None] - cumul[:, None, :], -jnp.inf))
    mixing = intersection[None] * decays
    scaled = inner.astype(jnp.float32) * steps.T[:, :, None]
    output = jnp.einsum("htj,jhd->thd", mixing, scaled, precision=highest)
    tail = jnp.exp(cumul[:, -1:] - cumul) * (segs == segs[-1]).astype(jnp.float32)[None, :]
    local_state = jnp.einsum(
        "ht,thd,tn->hdn", tail, scaled, read_b.astype(jnp.float32), precision=highest
    )
    through = jnp.exp(cumul[:, -1]) * (segs[-1] == prev_last).astype(jnp.float32)
    return (output, through, local_state, cumul)


def mamba_incoming(output, incoming, groups, segs, cumul, prev_last):
    read_c = groups[:, STATE_SIZE:].astype(jnp.float32)
    joined = (segs == prev_last).astype(jnp.float32)
    from_carry = jnp.einsum("hdn,tn->thd", incoming, read_c, precision=lax.Precision.HIGHEST)
    return output + jnp.exp(cumul).T[:, :, None] * joined[:, None, None] * from_carry


def combine_states(earlier, later):
    return (earlier[0] * later[0], later[0][:, None, None] * earlier[1] + later[1])


def shards(
    mamba_inner,
    mamba_groups,
    selective_gate,
    step_raw,
    step_bias,
    decay_log,
    conv_inner,
    conv_groups,
    gated_norm_gain,
    query_rows,
    key_rows,
    value_rows,
    segment_ids,
    mamba_proj,
    attn_proj,
):
    item_count = segment_ids.shape[0]
    taps = conv_inner.shape[0]
    resident_heads = step_raw.shape[0]
    rim_inner, rim_groups, rim_marks = shifted(
        (
            mamba_inner[item_count - taps + 1 :],
            mamba_groups[item_count - taps + 1 :],
            segment_ids[item_count - taps + 1 :].astype(jnp.bfloat16),
        ),
        "seq",
        1,
    )
    rim_segs = rim_marks.astype(jnp.float32).astype(jnp.int32)
    prev_last = rim_segs[-1]
    inner_filtered = conv_silu(mamba_inner, conv_inner, segment_ids, rim_inner, rim_segs).reshape(
        item_count, resident_heads, HEAD_CHANNELS
    )
    groups_conv = conv_silu(mamba_groups, conv_groups, segment_ids, rim_groups, rim_segs)
    steps = jax.nn.softplus(step_raw + step_bias[:, None])
    rates = jnp.exp(decay_log)
    output, through, local_state, cumul = mamba_local(
        inner_filtered, groups_conv, segment_ids, steps, rates, prev_last
    )
    identity = (jnp.ones_like(through), jnp.zeros_like(local_state))
    carry_decay, carry_state = entering((through, local_state), "seq", combine_states, identity)
    selective_output = mamba_incoming(
        output, carry_state, groups_conv, segment_ids, cumul, prev_last
    )
    gated_values = selective_output * jax.nn.silu(selective_gate.astype(jnp.float32)).reshape(
        item_count, resident_heads, HEAD_CHANNELS
    )
    mean_square = jnp.mean(gated_values * gated_values, axis=-1, keepdims=True)
    normalized_rows = (
        (
            gated_values
            * lax.rsqrt(mean_square + 1e-05)
            * gated_norm_gain.reshape(resident_heads, HEAD_CHANNELS)
        )
        .astype(jnp.bfloat16)
        .reshape(item_count, resident_heads * HEAD_CHANNELS)
    )
    heads_here = query_rows.shape[1] // HD
    group_size = QH // KVH
    kv_index = lax.axis_index("head") * heads_here // group_size
    my_keys = lax.dynamic_slice_in_dim(key_rows, kv_index * HD, HD, 1)
    my_values = lax.dynamic_slice_in_dim(value_rows, kv_index * HD, HD, 1)
    marks = segment_ids.astype(jnp.bfloat16)
    block_start = lax.axis_index("seq") * item_count
    query_pos = block_start + jnp.arange(item_count, dtype=jnp.int32)
    queries = query_rows.reshape(item_count, heads_here, HD).transpose(1, 0, 2)
    scale = 1.0 / math.sqrt(HD)
    start_state = (
        jnp.full((heads_here, item_count), -1e30, jnp.float32),
        jnp.zeros((heads_here, item_count), jnp.float32),
        jnp.zeros((heads_here, item_count, HD), jnp.float32),
    )
    piece_keys = lax.all_gather(my_keys, "seq", axis=0, tiled=True)
    piece_values = lax.all_gather(my_values, "seq", axis=0, tiled=True)
    piece_marks = lax.all_gather(marks, "seq", axis=0, tiled=True)
    rows = piece_keys.shape[0]
    width = math.gcd(rows, item_count)
    blocks = rows // width

    def one_block(state, item):
        top, total, summed = state
        block_keys, block_values, block_marks, offset = item
        key_pos = offset * width + jnp.arange(width, dtype=jnp.int32)
        key_seg = block_marks.astype(jnp.float32).astype(jnp.int32)
        allowed = (
            (key_seg[None, :] == segment_ids[:, None])
            & (key_pos[None, :] <= query_pos[:, None])
            & (key_pos[None, :] >= 0)
        )
        scores = (
            jnp.einsum("hqd,kd->hqk", queries, block_keys, preferred_element_type=jnp.float32)
            * scale
        )
        scores = jnp.where(allowed[None], scores, -jnp.inf)
        new_top = jnp.maximum(top, jnp.max(scores, axis=-1))
        rescale = jnp.exp(top - new_top)
        weights = jnp.exp(scores - new_top[..., None])
        total = total * rescale + jnp.sum(weights, axis=-1)
        summed = summed * rescale[..., None] + jnp.einsum(
            "hqk,kd->hqd",
            weights.astype(jnp.bfloat16),
            block_values,
            preferred_element_type=jnp.float32,
        )
        return ((new_top, total, summed), None)

    items = (
        piece_keys.reshape(blocks, width, HD),
        piece_values.reshape(blocks, width, HD),
        piece_marks.reshape(blocks, width),
        jnp.arange(blocks, dtype=jnp.int32),
    )
    result, unused = lax.scan(one_block, start_state, items)
    top_final, total_final, summed_final = result
    attended = (
        (summed_final / total_final[..., None])
        .astype(jnp.bfloat16)
        .transpose(1, 0, 2)
        .reshape(item_count, heads_here * HD)
    )
    terms = jnp.dot(normalized_rows, mamba_proj, preferred_element_type=jnp.float32) + jnp.dot(
        attended, attn_proj, preferred_element_type=jnp.float32
    )
    return lax.psum_scatter(terms.astype(jnp.bfloat16), "head", scatter_dimension=1, tiled=True)


def solution(mesh):
    placed = (
        P("seq", "head"),
        P("seq", None),
        P("seq", "head"),
        P("head", "seq"),
        P("head"),
        P("head"),
        P(None, "head"),
        P(),
        P("head"),
        P("seq", "head"),
        P("seq", None),
        P("seq", None),
        P("seq"),
        P("head", None),
        P("head", None),
    )
    return jax.shard_map(
        shards, mesh=mesh, in_specs=placed, out_specs=P("seq", "head"), check_vma=False
    )
```

profile of v0, /device:TPU:0, one launch (start us, length us, event | category | flops | bytes accessed | tf_op | source)
XLA Modules:
  0.0 241.9 jit_solution(1705443980735956197)
XLA Ops:
  7.9 5.4 %collective-permute-start.1 = (bf16[3]{0:T(256)(128)(2,1)}, bf16[3]{0:T(256)(128)(2,1)}, u32[]{:S(2)}, u32[]{:S(2)}) collective-permute-start(bf16[3]{0:T(256)(128)(2,1)} %slice.85), channel_id=1, source_target_pairs={{0,4},{4,8},{8,12},{12,16},{16,20},{20,24},{24,28},{1,5},{5,9},{9,... | collective-permute-start | bytes 26 | tf_op jit(solution)/shard_map/ppermute | solution.py:17
  14.0 3.5 %collective-permute-start.2 = (bf16[3,512]{1,0:T(4,128)(2,1)S(1)}, bf16[3,512]{1,0:T(4,128)(2,1)}, u32[]{:S(2)}, u32[]{:S(2)}) collective-permute-start(bf16[3,512]{1,0:T(4,128)(2,1)S(1)} %slice.95), channel_id=1, source_target_pairs={{0,4},{4,8},{8,12},{12,16},{16,20},{20,24},{24,28},{1,5},{5,9},{9,... | collective-permute-start | bytes 9224 | tf_op jit(solution)/shard_map/ppermute | solution.py:17
  19.1 3.5 %collective-permute-start = (bf16[3,768]{0,1:T(8,128)(2,1)}, bf16[3,768]{0,1:T(8,128)(2,1)}, u32[]{:S(2)}, u32[]{:S(2)}) collective-permute-start(bf16[3,768]{0,1:T(8,128)(2,1)} %copy.27), channel_id=1, source_target_pairs={{0,4},{4,8},{8,12},{12,16},{16,20},{20,24},{24,28},{1,5},{5,9},{9,... | collective-permute-start | bytes 13832 | tf_op jit(solution)/shard_map/ppermute | solution.py:17
  31.8 32.9 %all_gather.23 = bf16[1024,128]{1,0:T(8,128)(2,1)} all-gather(bf16[128,128]{1,0:T(8,128)(2,1)S(1)} %constant_dynamic-slice_fusion.2), channel_id=1, replica_groups=mesh['seq'=8,'head'=4] {'seq'}, dimensions={0}, use_global_device_ids=true | all-gather | bytes 294912 | tf_op jit(solution)/shard_map/all_gather | solution.py:159
  65.5 32.9 %all_gather.24 = bf16[1024,128]{1,0:T(8,128)(2,1)} all-gather(bf16[128,128]{1,0:T(8,128)(2,1)S(1)} %constant_dynamic-slice_fusion.1), channel_id=1, replica_groups=mesh['seq'=8,'head'=4] {'seq'}, dimensions={0}, use_global_device_ids=true | all-gather | bytes 294912 | tf_op jit(solution)/shard_map/all_gather | solution.py:160
  98.4 16.8 %all-gather.2 = bf16[8,1,128]{2,1,0:T(2,128)(2,1)S(1)} all-gather(bf16[1,1,128]{2,1,0:T(2,128)(2,1)S(1)} %get-tuple-element.295), channel_id=1, replica_groups=mesh['seq'=8,'head'=4] {'seq'}, dimensions={0}, use_global_device_ids=true | all-gather | bytes 2304 | tf_op jit(solution)/shard_map/all_gather | solution.py:161
  118.8 2.0 compare_convert_fusion.4
  124.7 2.5 %multiply_convert_fusion.1 = bf16[128,768]{0,1:T(8,128)(2,1)S(1)} fusion(f32[128,768]{0,1:T(8,128)} %convert_element_type.121, f32[3,768]{0,1:T(8,128)S(1)} %convert_element_type.120, f32[768]{0:T(1024)S(1)} %get-tuple-element.241, f32[128]{0:T(128)S(1)} %get-tuple-element.290, f32[768]{0:T(1024)S(1)} %get-tuple-element.242, f32[128]{0:T(128)S(1)} %get-tuple-element.291, ...), kind=kLoop, calls=%fused_computation.74 | loop fusion | flops 1769472 | bytes 612864 | tf_op jit(solution)/shard_map/convert_element_type | solution.py:52
  129.2 32.5 %while.30 = (s32[]{:T(128)}, f32[2,128]{1,0:T(2,128)S(1)}, f32[2,128]{1,0:T(2,128)S(1)}, f32[2,128,128]{2,1,0:T(8,128)S(1)}, bf16[8,128]{1,0:T(8,128)(2,1)}, /*i...) while((s32[]{:T(128)}, f32[2,128]{1,0:T(2,128)S(1)}, ...), condition=%wide.region_7.8_spmd.clone, body=%wide.region_4.7_spmd.clone.sunk | while | flops 17172484 | bytes 840889 | solution.py:199
  161.7 1.8 copy.29
  166.4 1.8 convert_multiply_fusion
  168.2 2.6 %fusion.76 = f32[128,2048]{1,0:T(8,128)} fusion(bf16[128,256]{0,1:T(8,128)(2,1)S(1)} %bitcast.93, bf16[256,2048]{1,0:T(8,128)(2,1)} %param.33), kind=kOutput, calls=%fused_computation.132 | convolution fusion | flops 134217728 | bytes 2162688 | tf_op jit(solution)/shard_map/dot_general | solution.py:207
  172.5 18.7 %all-reduce = bf16[96]{0:T(256)(128)(2,1)S(1)} all-reduce(bf16[96]{0:T(256)(128)(2,1)S(1)} %dynamic-update-slice), channel_id=2, replica_groups=mesh['seq'=8,'head'=4] {'seq'}, use_global_device_ids=true, to_apply=%add | all-reduce | flops 96 | bytes 384
  191.4 18.2 %while.29 = (s32[]{:T(128)}, f32[12,64,256]{2,1,0:T(8,128)}, s32[]{:T(128)}, bf16[8,12]{1,0:T(8,128)(2,1)S(1)}, bf16[8,12,64,256]{3,2,1,0:T(8,128)(2,1)}, /*index=5*/s32[]{:T(128)}, s32[]{:T(128)}) while((s32[]{:T(128)}, f32[12,64,256]{2,1,0:T(8,128)}, s32[]{:T(128)}, bf16[8,12]{1,0:T(8,128)(2,1)S(1)}, ...), condition=%wide.region_2.3_spmd.clone, body=%wide.region_1.2_spmd.clone.sunk | while | flops 983056 | bytes 1966305 | solution.py:40
  191.5 2.1 fusion.92
  193.5 2.3 fusion.92
  195.8 2.3 fusion.92
  198.1 2.3 fusion.92
  200.4 2.3 fusion.92
  202.7 2.3 fusion.92
  205.0 2.3 fusion.92
  207.3 2.3 fusion.92
  211.3 2.8 %multiply_reduce_fusion = (f32[128,12]{0,1:T(8,128)S(1)}, f32[128,12,64]{0,2,1:T(8,128)S(1)}) fusion(f32[128,12,64]{0,2,1:T(8,128)} %bitcast.92, f32[128,12,64]{0,2,1:T(8,128)S(1)} %convolution_multiply_fusion.1, f32[12,128]{1,0:T(8,128)S(1)} %reduce_window_sum.11, f32[128,128]{1,0:T(8,128)S(1)} %fusion.66, pred[128,128]{1,0:T(8,128)(4,1)S(1)} %fusion.64, ...), kind=kOutput, calls=%fused_computation.69 | convolution fusion | flops 152173056 | bytes 1476608 | tf_op jit(solution)/shard_map/htj,jhd->thd/dot_general | solution.py:66
  215.8 19.3 %reduce-scatter.2.cloned.1.call-done = bf16[128,512]{1,0:T(8,128)(2,1)} async-done(((bf16[128,2048]{1,0:T(8,128)(2,1)}), bf16[128,512]{1,0:T(8,128)(2,1)}) %reduce-scatter.2.cloned.1.call-update) | async-done | bytes 131088 | tf_op jit(solution)/shard_map/reduce_scatter | solution.py:210
  (173 shorter events, 56.6 us)
Async XLA Ops:
  6.5 207.8 %copy-start = (bf16[768,2048]{1,0:T(8,128)(2,1)S(1)}, bf16[768,2048]{1,0:T(8,128)(2,1)}, u32[]{:S(2)}) copy-start(bf16[768,2048]{1,0:T(8,128)(2,1)} %param.32) | copy-start | bytes 9437188
  6.5 122.6 %copy-start.5 = (s32[128]{0:T(128)S(1)}, s32[128]{0:T(128)}, u32[]{:S(2)}) copy-start(s32[128]{0:T(128)} %param.31) | copy-start | bytes 1540
  6.5 184.9 %all-gather.5.cloned.1.call-start = ((), (), s32[]{:S(2)}) async-start(), calls=%async_computation.2 | async-start | bytes 3538944 | tf_op jit(solution)/shard_map/all_gather | solution.py:23
  7.9 108.9 %collective-permute-start.1 = (bf16[3]{0:T(256)(128)(2,1)}, bf16[3]{0:T(256)(128)(2,1)}, u32[]{:S(2)}, u32[]{:S(2)}) collective-permute-start(bf16[3]{0:T(256)(128)(2,1)} %slice.85), channel_id=1, source_target_pairs={{0,4},{4,8},{8,12},{12,16},{16,20},{20,24},{24,28},{1,5},{5,9},{9,... | collective-permute-start | bytes 26 | tf_op jit(solution)/shard_map/ppermute | solution.py:17
  14.0 107.4 %collective-permute-start.2 = (bf16[3,512]{1,0:T(4,128)(2,1)S(1)}, bf16[3,512]{1,0:T(4,128)(2,1)}, u32[]{:S(2)}, u32[]{:S(2)}) collective-permute-start(bf16[3,512]{1,0:T(4,128)(2,1)S(1)} %slice.95), channel_id=1, source_target_pairs={{0,4},{4,8},{8,12},{12,16},{16,20},{20,24},{24,28},{1,5},{5,9},{9,... | collective-permute-start | bytes 9224 | tf_op jit(solution)/shard_map/ppermute | solution.py:17
  19.1 104.6 %collective-permute-start = (bf16[3,768]{0,1:T(8,128)(2,1)}, bf16[3,768]{0,1:T(8,128)(2,1)}, u32[]{:S(2)}, u32[]{:S(2)}) collective-permute-start(bf16[3,768]{0,1:T(8,128)(2,1)} %copy.27), channel_id=1, source_target_pairs={{0,4},{4,8},{8,12},{12,16},{16,20},{20,24},{24,28},{1,5},{5,9},{9,... | collective-permute-start | bytes 13832 | tf_op jit(solution)/shard_map/ppermute | solution.py:17
  30.6 98.6 %copy-start.6 = (f32[128,12]{0,1:T(8,128)}, f32[128,12]{0,1:T(8,128)S(1)}, u32[]{:S(2)}) copy-start(f32[128,12]{0,1:T(8,128)S(1)} %get-tuple-element.281) | copy-start | bytes 18436
  123.7 3.5 %copy-start.2 = (bf16[128,512]{1,0:T(8,128)(2,1)}, bf16[128,512]{1,0:T(8,128)(2,1)S(1)}, u32[]{:S(2)}) copy-start(bf16[128,512]{1,0:T(8,128)(2,1)S(1)} %multiply_convert_fusion.2) | copy-start | bytes 393220
  127.2 0.7 copy-start.4
  127.2 36.3 %copy-start.10 = (f32[768]{0:T(1024)S(1)}, f32[768]{0:T(1024)}, u32[]{:S(2)}) copy-start(f32[768]{0:T(1024)} %param.27) | copy-start | bytes 9220
  129.1 106.0 %reduce-scatter.2.cloned.1.call-start = ((), (), s32[]{:S(2)}) async-start(), calls=%async_computation.1 | async-start | bytes 655360 | tf_op jit(solution)/shard_map/reduce_scatter | solution.py:210
  161.7 29.6 %copy-start.3 = (bf16[128,512]{1,0:T(8,128)(2,1)S(1)}, bf16[128,512]{1,0:T(8,128)(2,1)}, u32[]{:S(2)}) copy-start(bf16[128,512]{1,0:T(8,128)(2,1)} %copy-done.2) | copy-start | bytes 393220
  191.4 18.2 %copy-start.8 = (f32[128,12]{0,1:T(8,128)S(1)}, f32[128,12]{0,1:T(8,128)}, u32[]{:S(2)}) copy-start(f32[128,12]{0,1:T(8,128)} %get-tuple-element.283) | copy-start | bytes 18436
  191.4 19.9 %copy-start.7 = (f32[128,12]{0,1:T(8,128)S(1)}, f32[128,12]{0,1:T(8,128)}, u32[]{:S(2)}) copy-start(f32[128,12]{0,1:T(8,128)} %copy-done.6) | copy-start | bytes 18436
  191.4 22.7 %copy-start.9 = (f32[12,64]{1,0:T(8,128)S(1)}, f32[12,64]{1,0:T(8,128)}, u32[]{:S(2)}) copy-start(f32[12,64]{1,0:T(8,128)} %mul.345) | copy-start | bytes 9220
  209.6 4.7 %copy-start.1 = (f32[128,2048]{1,0:T(8,128)S(1)}, f32[128,2048]{1,0:T(8,128)}, u32[]{:S(2)}) copy-start(f32[128,2048]{1,0:T(8,128)} %fusion.76) | copy-start | bytes 3145732
Sparse Core Ops, SparseCore 0:
  129.2 58.6 all-gather.4
  215.9 19.1 reduce-scatter.1
where the time goes:
time: 244 us; the launch traced here: 242 us
  blocking collectives  101 us (41%)
  other arithmetic  41.5 us (17%)
  matrix products  25.3 us (10%)
  local copies, waits for them, and re-layouts  21.2 us (9%)
  waiting for transfers between devices  19.4 us (8%)
  between operations  15.7 us (6%)
  starting transfers between devices  12.4 us (5%)
  loops' own time  5.2 us (2%)
    all_gather x1, blocking collectives, shards(): piece_keys = lax.all_gather(my_keys, 'seq', axis=0, tiled=True)  32.9 us
    all_gather x1, blocking collectives, shards(): piece_values = lax.all_gather(my_values, 'seq', axis=0, tiled=True)  32.9 us
    reduce_scatter x1, waiting for transfers between devices, shards(): lax.psum_scatter(terms.astype(jnp.bfloat16), 'head', scatter_dimension=1,...  19.3 us
    unnamed x1, blocking collectives  18.7 us
    select_n x8, other arithmetic, turn(): return jax.tree.map(lambda a, b: jnp.where(reached, a, b), new, before)  18.1 us
    all_gather x1, blocking collectives, shards(): piece_marks = lax.all_gather(marks, 'seq', axis=0, tiled=True)  16.8 us
    ppermute x3, starting transfers between devices, shifted(): lax.ppermute(value, axis, [(source, source + steps) for source in range(f...  12.4 us
    dot_general x8, matrix products, one_block(): jnp.einsum('hqk,kd->hqd', weights.astype(jnp.bfloat16), block_values, pre...  7.87 us
  transfers between devices with their start and end apart: 5, of which 1 were waited for; matrix products, arithmetic and copies ran while one was open for 24% of the time, Pallas kernels for 0%

commit v1 on v0

--- a/solution.py
+++ b/solution.py
@@ -156,7 +156,14 @@
         jnp.zeros((heads_here, item_count), jnp.float32),
         jnp.zeros((heads_here, item_count, HD), jnp.float32),
     )
-    piece_keys = lax.all_gather(my_keys, "seq", axis=0, tiled=True)
+    ways, here, step = (lax.axis_size("seq"), lax.axis_index("seq"), my_keys.shape[0])
+    line, have = (my_keys, 1)
+    while have < ways:
+        line = jnp.concatenate(
+            [line, lax.ppermute(line, "seq", [(d, (d - have) % ways) for d in range(ways)])], axis=0
+        )
+        have = 2 * have
+    piece_keys = jnp.roll(line, here * step, axis=0)
     piece_values = lax.all_gather(my_values, "seq", axis=0, tiled=True)
     piece_marks = lax.all_gather(marks, "seq", axis=0, tiled=True)
     rows = piece_keys.shape[0]

time: 244 us -> 255 us (1.045)
  blocking collectives: 101 us -> 68.5 us
  other arithmetic: 41.5 us -> 63.4 us
  waiting for transfers between devices: 19.4 us -> 29.6 us
  local copies, waits for them, and re-layouts: 21.2 us -> 30.4 us
    all_gather x1 -> x0, blocking collectives: 32.9 us -> none  [shards(): piece_keys = lax.all_gather(my_keys, 'seq', axis=0, tiled=True)]
    convert_element_type x8, other arithmetic: 0.04 us -> 10.3 us  [turn(): part[k].astype(own.dtype)]
    add x8, other arithmetic: 0.14 us -> 9.6 us  [one_block(): total = total * rescale + jnp.sum(weights, axis=-1)]
    ppermute x0 -> x3, waiting for transfers between devices: none -> 6.91 us  [shards(): lax.ppermute(line, 'seq', [(d, (d - have) % ways) for d in range(ways)])]
    unnamed x30 -> x33, local copies, waits for them, and re-layouts: 6.8 us -> 10.8 us
  transfers between devices with their start and end apart: 5 -> 8, of which waited for: 1 -> 4; matrix products, arithmetic and copies ran while one was open for 24% -> 33% of each run, Pallas kernels for 0% -> 0%
where the time goes in v1:
time: 255 us; the launch traced here: 252 us
  blocking collectives  68.5 us (27%)
  other arithmetic  63.4 us (25%)
  local copies, waits for them, and re-layouts  30.4 us (12%)
  waiting for transfers between devices  29.6 us (12%)
  matrix products  26.5 us (10%)
  between operations  15.5 us (6%)
  starting transfers between devices  12.8 us (5%)
  loops' own time  5.08 us (2%)
    all_gather x1, blocking collectives, shards(): piece_values = lax.all_gather(my_values, 'seq', axis=0, tiled=True)  32.8 us
    reduce_scatter x1, waiting for transfers between devices, shards(): lax.psum_scatter(terms.astype(jnp.bfloat16), 'head', scatter_dimension=1,...  20.6 us
    all_gather x1, blocking collectives, shards(): piece_marks = lax.all_gather(marks, 'seq', axis=0, tiled=True)  18.5 us
    select_n x8, other arithmetic, turn(): return jax.tree.map(lambda a, b: jnp.where(reached, a, b), new, before)  18.2 us
    unnamed x1, blocking collectives  17.2 us
    ppermute x3, starting transfers between devices, shifted(): lax.ppermute(value, axis, [(source, source + steps) for source in range(f...  12.4 us
    unnamed x33, local copies, waits for them, and re-layouts  10.8 us
    convert_element_type x8, other arithmetic, turn(): part[k].astype(own.dtype)  10.3 us
  transfers between devices with their start and end apart: 8, of which 4 were waited for; matrix products, arithmetic and copies ran while one was open for 33% of the time, Pallas kernels for 0%

profile of v1, /device:TPU:0, one launch (start us, length us, event | category | flops | bytes accessed | tf_op | source)
XLA Modules:
  0.0 251.7 jit_solution(2249490985111721678)
XLA Ops:
  8.5 5.4 %collective-permute-start.1 = (bf16[3]{0:T(256)(128)(2,1)}, bf16[3]{0:T(256)(128)(2,1)}, u32[]{:S(2)}, u32[]{:S(2)}) collective-permute-start(bf16[3]{0:T(256)(128)(2,1)} %slice.85), channel_id=1, source_target_pairs={{0,4},{4,8},{8,12},{12,16},{16,20},{20,24},{24,28},{1,5},{5,9},{9,... | collective-permute-start | bytes 26 | tf_op jit(solution)/shard_map/ppermute | solution.py:17
  15.2 3.5 %collective-permute-start.2 = (bf16[3,512]{1,0:T(4,128)(2,1)}, bf16[3,512]{1,0:T(4,128)(2,1)}, u32[]{:S(2)}, u32[]{:S(2)}) collective-permute-start(bf16[3,512]{1,0:T(4,128)(2,1)} %slice.95), channel_id=1, source_target_pairs={{0,4},{4,8},{8,12},{12,16},{16,20},{20,24},{24,28},{1,5},{5,9},{9,... | collective-permute-start | bytes 9224 | tf_op jit(solution)/shard_map/ppermute | solution.py:17
  20.3 3.5 %collective-permute-start = (bf16[3,768]{0,1:T(8,128)(2,1)}, bf16[3,768]{0,1:T(8,128)(2,1)}, u32[]{:S(2)}, u32[]{:S(2)}) collective-permute-start(bf16[3,768]{0,1:T(8,128)(2,1)} %copy.27), channel_id=1, source_target_pairs={{0,4},{4,8},{8,12},{12,16},{16,20},{20,24},{24,28},{1,5},{5,9},{9,... | collective-permute-start | bytes 13832 | tf_op jit(solution)/shard_map/ppermute | solution.py:17
  41.3 32.8 %all_gather.20 = bf16[1024,128]{1,0:T(8,128)(2,1)} all-gather(bf16[128,128]{1,0:T(8,128)(2,1)S(1)} %constant_dynamic-slice_fusion.1), channel_id=1, replica_groups=mesh['seq'=8,'head'=4] {'seq'}, dimensions={0}, use_global_device_ids=true | all-gather | bytes 294912 | tf_op jit(solution)/shard_map/all_gather | solution.py:167
  74.2 18.5 %all-gather.2 = bf16[8,1,128]{2,1,0:T(2,128)(2,1)S(1)} all-gather(bf16[1,1,128]{2,1,0:T(2,128)(2,1)} %get-tuple-element.297), channel_id=1, replica_groups=mesh['seq'=8,'head'=4] {'seq'}, dimensions={0}, use_global_device_ids=true | all-gather | bytes 2304 | tf_op jit(solution)/shard_map/all_gather | solution.py:168
  101.8 17.2 %all-reduce = bf16[96]{0:T(256)(128)(2,1)S(1)} all-reduce(bf16[96]{0:T(256)(128)(2,1)S(1)} %dynamic-update-slice), channel_id=2, replica_groups=mesh['seq'=8,'head'=4] {'seq'}, use_global_device_ids=true, to_apply=%add | all-reduce | flops 96 | bytes 384
  123.6 2.5 %multiply_convert_fusion.1 = bf16[128,768]{0,1:T(8,128)(2,1)S(1)} fusion(f32[128,768]{0,1:T(8,128)} %convert_element_type.121, f32[3,768]{0,1:T(8,128)S(1)} %convert_element_type.120, f32[768]{0:T(1024)} %get-tuple-element.241, f32[128]{0:T(128)S(1)} %get-tuple-element.292, f32[768]{0:T(1024)} %get-tuple-element.242, f32[128]{0:T(128)S(1)} %get-tuple-element.293, ...), kind=kLoop, calls=%fused_computation.74 | loop fusion | flops 1769472 | bytes 612864 | tf_op jit(solution)/shard_map/convert_element_type | solution.py:52
  126.8 1.9 convolution_convert_fusion
  131.8 5.3 %collective-permute-done.5 = bf16[512,128]{1,0:T(8,128)(2,1)S(1)} collective-permute-done((bf16[512,128]{1,0:T(8,128)(2,1)S(1)}, bf16[512,128]{1,0:T(8,128)(2,1)S(1)}, u32[]{:S(2)}, u32[]{:S(2)}) %collective-permute-start.5) | collective-permute-done | bytes 131104 | tf_op jit(solution)/shard_map/ppermute | solution.py:163
  141.8 41.7 %while.30 = (s32[]{:T(128)}, f32[2,128]{1,0:T(2,128)S(1)}, f32[2,128]{1,0:T(2,128)}, f32[2,128,128]{2,1,0:T(8,128)S(1)}, bf16[8,128]{1,0:T(8,128)(2,1)}, /*index...) while((s32[]{:T(128)}, f32[2,128]{1,0:T(2,128)S(1)}, ...), condition=%wide.region_7.8_spmd.clone, body=%wide.region_4.7_spmd.clone.sunk | while | flops 17172484 | bytes 840889 | solution.py:206
  184.3 2.5 %fusion.76 = f32[128,2048]{1,0:T(8,128)} fusion(bf16[128,256]{0,1:T(8,128)(2,1)S(1)} %bitcast.93, bf16[256,2048]{1,0:T(8,128)(2,1)} %param.33), kind=kOutput, calls=%fused_computation.143 | convolution fusion | flops 134217728 | bytes 2162688 | tf_op jit(solution)/shard_map/dot_general | solution.py:214
  186.9 2.1 all-gather.5.cloned.1.call-done
  188.9 28.5 %while.29 = (s32[]{:T(128)}, f32[12,64,256]{2,1,0:T(8,128)}, s32[]{:T(128)}, bf16[8,12]{1,0:T(8,128)(2,1)}, bf16[8,12,64,256]{3,2,1,0:T(8,128)(2,1)}, /*index=5*/s32[]{:T(128)}, s32[]{:T(128)}) while((s32[]{:T(128)}, f32[12,64,256]{2,1,0:T(8,128)}, s32[]{:T(128)}, bf16[8,12]{1,0:T(8,128)(2,1)}, bf16[8,12,64,256]{3,2,1,0:T(8,128)(2,1)}, ...), condition=%wide.region_2.3_spmd.clone, body=%wide.region_1.2_spmd.clone.sunk | while | flops 983056 | bytes 1966305 | solution.py:40
  190.3 2.1 fusion.92
  193.6 2.3 fusion.92
  197.2 2.3 fusion.92
  200.8 2.3 fusion.92
  204.4 2.3 fusion.92
  208.0 2.3 fusion.92
  211.6 2.3 fusion.92
  215.2 2.3 fusion.92
  217.5 1.7 convolution_multiply_fusion.1
  219.2 2.7 %multiply_reduce_fusion = (f32[128,12]{0,1:T(8,128)S(1)}, f32[128,12,64]{0,2,1:T(8,128)S(1)}) fusion(f32[128,12,64]{0,2,1:T(8,128)} %bitcast.92, f32[128,12,64]{0,2,1:T(8,128)S(1)} %convolution_multiply_fusion.1, f32[12,128]{1,0:T(8,128)S(1)} %reduce_window_sum.11, f32[128,128]{1,0:T(8,128)S(1)} %copy-done.6, pred[128,128]{1,0:T(8,128)(4,1)} %fusion.64, ...), kind=kOutput, calls=%fused_computation.69 | convolution fusion | flops 152173056 | bytes 1476608 | tf_op jit(solution)/shard_map/htj,jhd->thd/dot_general | solution.py:66
  224.3 20.6 %reduce-scatter.2.cloned.1.call-done = bf16[128,512]{1,0:T(8,128)(2,1)} async-done(((bf16[128,2048]{1,0:T(8,128)(2,1)}), bf16[128,512]{1,0:T(8,128)(2,1)}) %reduce-scatter.2.cloned.1.call-update) | async-done | bytes 131088 | tf_op jit(solution)/shard_map/reduce_scatter | solution.py:217
  (184 shorter events, 92.7 us)
Async XLA Ops:
  6.5 216.3 %copy-start = (bf16[768,2048]{1,0:T(8,128)(2,1)S(1)}, bf16[768,2048]{1,0:T(8,128)(2,1)}, u32[]{:S(2)}) copy-start(bf16[768,2048]{1,0:T(8,128)(2,1)} %param.32) | copy-start | bytes 9437188
  6.5 91.0 %copy-start.7 = (s32[128]{0:T(128)S(1)}, s32[128]{0:T(128)}, u32[]{:S(2)}) copy-start(s32[128]{0:T(128)} %param.31) | copy-start | bytes 1540
  6.5 182.4 %all-gather.5.cloned.1.call-start = ((), (), s32[]{:S(2)}) async-start(), calls=%async_computation.2 | async-start | bytes 3538944 | tf_op jit(solution)/shard_map/all_gather | solution.py:23
  8.5 87.7 %collective-permute-start.1 = (bf16[3]{0:T(256)(128)(2,1)}, bf16[3]{0:T(256)(128)(2,1)}, u32[]{:S(2)}, u32[]{:S(2)}) collective-permute-start(bf16[3]{0:T(256)(128)(2,1)} %slice.85), channel_id=1, source_target_pairs={{0,4},{4,8},{8,12},{12,16},{16,20},{20,24},{24,28},{1,5},{5,9},{9,... | collective-permute-start | bytes 26 | tf_op jit(solution)/shard_map/ppermute | solution.py:17
  15.2 104.4 %collective-permute-start.2 = (bf16[3,512]{1,0:T(4,128)(2,1)}, bf16[3,512]{1,0:T(4,128)(2,1)}, u32[]{:S(2)}, u32[]{:S(2)}) collective-permute-start(bf16[3,512]{1,0:T(4,128)(2,1)} %slice.95), channel_id=1, source_target_pairs={{0,4},{4,8},{8,12},{12,16},{16,20},{20,24},{24,28},{1,5},{5,9},{9,... | collective-permute-start | bytes 9224 | tf_op jit(solution)/shard_map/ppermute | solution.py:17
  20.3 102.3 %collective-permute-start = (bf16[3,768]{0,1:T(8,128)(2,1)}, bf16[3,768]{0,1:T(8,128)(2,1)}, u32[]{:S(2)}, u32[]{:S(2)}) collective-permute-start(bf16[3,768]{0,1:T(8,128)(2,1)} %copy.27), channel_id=1, source_target_pairs={{0,4},{4,8},{8,12},{12,16},{16,20},{20,24},{24,28},{1,5},{5,9},{9,... | collective-permute-start | bytes 13832 | tf_op jit(solution)/shard_map/ppermute | solution.py:17
  25.2 100.9 %collective-permute-start.3 = (bf16[128,128]{1,0:T(8,128)(2,1)S(1)}, bf16[128,128]{1,0:T(8,128)(2,1)S(1)}, u32[]{:S(2)}, u32[]{:S(2)}) collective-permute-start(bf16[128,128]{1,0:T(8,128)(2,1)S(1)} %get-tuple-element.278), channel_id=1, source_target_pairs={{0,28},{4,0},{8,4},{12,8},{16,12},{20,16},{24,20},{28,24},{1,29},{... | collective-permute-start | bytes 98312 | tf_op jit(solution)/shard_map/ppermute | solution.py:163
  121.8 4.6 %copy-start.2 = (bf16[128,512]{1,0:T(8,128)(2,1)}, bf16[128,512]{1,0:T(8,128)(2,1)S(1)}, u32[]{:S(2)}) copy-start(bf16[128,512]{1,0:T(8,128)(2,1)S(1)} %multiply_convert_fusion.2) | copy-start | bytes 393220
  126.1 0.7 copy-start.4
  126.1 4.3 %collective-permute-start.4 = (bf16[256,128]{1,0:T(8,128)(2,1)S(1)}, bf16[256,128]{1,0:T(8,128)(2,1)S(1)}, u32[]{:S(2)}, u32[]{:S(2)}) collective-permute-start(bf16[256,128]{1,0:T(8,128)(2,1)S(1)} %pad_maximum_fusion.3), channel_id=1, source_target_pairs={{0,24},{4,28},{8,0},{12,4},{16,8},{20,12},{24,16},{28,20},{1,25},{... | collective-permute-start | bytes 196616 | tf_op jit(solution)/shard_map/ppermute | solution.py:163
  128.7 116.1 %reduce-scatter.2.cloned.1.call-start = ((), (), s32[]{:S(2)}) async-start(), calls=%async_computation.1 | async-start | bytes 655360 | tf_op jit(solution)/shard_map/reduce_scatter | solution.py:217
  130.5 6.6 %collective-permute-start.5 = (bf16[512,128]{1,0:T(8,128)(2,1)S(1)}, bf16[512,128]{1,0:T(8,128)(2,1)S(1)}, u32[]{:S(2)}, u32[]{:S(2)}) collective-permute-start(bf16[512,128]{1,0:T(8,128)(2,1)S(1)} %pad_maximum_fusion.2), channel_id=1, source_target_pairs={{0,16},{4,20},{8,24},{12,28},{16,0},{20,4},{24,8},{28,12},{1,17},{... | collective-permute-start | bytes 393224 | tf_op jit(solution)/shard_map/ppermute | solution.py:163
  188.9 28.5 %copy-start.3 = (bf16[128,512]{1,0:T(8,128)(2,1)S(1)}, bf16[128,512]{1,0:T(8,128)(2,1)}, u32[]{:S(2)}) copy-start(bf16[128,512]{1,0:T(8,128)(2,1)} %copy-done.2) | copy-start | bytes 393220
  188.9 30.3 %copy-start.5 = (bf16[128,768]{0,1:T(8,128)(2,1)S(1)}, bf16[128,768]{0,1:T(8,128)(2,1)}, u32[]{:S(2)}) copy-start(bf16[128,768]{0,1:T(8,128)(2,1)} %copy-done.4) | copy-start | bytes 589828
  188.9 30.3 %copy-start.6 = (f32[128,128]{1,0:T(8,128)S(1)}, f32[128,128]{1,0:T(8,128)}, u32[]{:S(2)}) copy-start(f32[128,128]{1,0:T(8,128)} %fusion.66) | copy-start | bytes 196612
  188.9 30.3 %copy-start.8 = (f32[128,12]{0,1:T(8,128)S(1)}, f32[128,12]{0,1:T(8,128)}, u32[]{:S(2)}) copy-start(f32[128,12]{0,1:T(8,128)} %get-tuple-element.283) | copy-start | bytes 18436
  217.5 5.4 %copy-start.1 = (f32[128,2048]{1,0:T(8,128)S(1)}, f32[128,2048]{1,0:T(8,128)}, u32[]{:S(2)}) copy-start(f32[128,2048]{1,0:T(8,128)} %fusion.76) | copy-start | bytes 3145732
Sparse Core Ops, SparseCore 0:
  128.9 60.0 all-gather.4
  224.4 20.4 reduce-scatter.1
